TPU v7x, 32 devices: a whole 2x2x4 slice. The times are simulated.
32 devices in a mesh: row: 8 (over y, x, core), col: 4 (over z).
Axes of the slice: x: 2, y: 2, z: 4, core: 2. Of those that a mesh axis runs over, the one named last changes fastest.
Arguments:
- covariance: float32 [2048, 2048], P('row', 'col'), may hold values from 0 to 4, as said below
- panels: int32 [4], replicated, may hold values from 0 to 7, as said below
- observed: float32 [2048], P('row'), may hold values from -6 to 6
- drift_basis: float32 [64, 2048], P(None, 'row'), may hold values from -1.5 to 1.5
Outputs:
- complement: float32 [2048, 2048], P('row', 'col')
- factor: float32 [2048, 1024], P('row')
- solved_data: float32 [2048], P('row')
- solved_drift: float32 [64, 2048], P(None, 'row')
Inputs may be any that keep to these rules, and one draw needn't show every extreme that they name: `covariance`: symmetric and positive definite. `panels`: 4 different tile indices; tile 8 - 1 is always among them.
All inputs are finite; a program needn't handle non-finite values.
Results may differ from a plain program's by a relative error of at most 0.0003.
Values sent between devices are 32-bit elements; how exact they have to be, the bound alone decides.
A program may use at most 64 MiB of HBM per device.

v0:
```python
import jax
import jax.numpy as jnp
from jax import lax
from jax.sharding import PartitionSpec as P

B = 256
K = 4


def broadcast(value, axis, root):
    mine = lax.axis_index(axis) == root
    return lax.psum(jnp.where(mine, value, jnp.zeros_like(value)), axis)


def solve_right(chol_tile, values):
    return lax.linalg.triangular_solve(
        chol_tile, values, left_side=False, lower=True, transpose_a=True
    )


def keep_mask(tiles, chosen):
    return jnp.all(tiles[:, None] != chosen[None, :], axis=1).astype(jnp.float32)


def outer_product(rows_factor, cols_factor):
    return lax.dot_general(
        rows_factor, cols_factor, (((1,), (0,)), ((), ())), precision=lax.Precision.HIGHEST
    )


def on_device(covariance, panels, observed, drift_basis):
    rows_here = covariance.shape[0]
    cols_here = covariance.shape[1]
    row_start = lax.axis_index("row") * rows_here
    col_start = lax.axis_index("col") * cols_here
    row_tiles = (row_start + lax.iota(jnp.int32, rows_here)) // B
    col_tiles = (col_start + lax.iota(jnp.int32, cols_here)) // B
    sides = jnp.concatenate([observed[None, :], drift_basis], axis=0)
    matrix = covariance
    factors = []
    for position in range(K):
        target = panels[position]
        offset = target * B
        row_owner = offset // rows_here
        col_owner = offset // cols_here
        col_off = offset - col_owner * cols_here
        keep_rows = keep_mask(row_tiles, panels[:position])
        keep_cols = keep_mask(col_tiles, panels[:position])
        col_slab = lax.dynamic_slice_in_dim(matrix, col_off, B, 1)
        col_slab = broadcast(col_slab, "col", col_owner)
        side_tile = sides
        diag_tile = col_slab
        row_slab = matrix
        row_slab, diag_tile, side_tile = (
            broadcast(row_slab, "row", row_owner),
            broadcast(diag_tile, "row", row_owner),
            broadcast(side_tile, "row", row_owner),
        )
        chol_tile = jnp.linalg.cholesky(diag_tile)
        rows_factor = solve_right(chol_tile, col_slab) * keep_rows[:, None]
        cols_factor = (
            lax.linalg.triangular_solve(
                chol_tile, row_slab, left_side=True, lower=True, transpose_a=False
            )
            * keep_cols[None, :]
        )
        solved = solve_right(chol_tile, side_tile)
        matrix = matrix - outer_product(rows_factor, cols_factor)
        sides = sides - lax.dot_general(
            solved, rows_factor, (((1,), (1,)), ((), ())), precision=lax.Precision.HIGHEST
        )
        sides = jnp.where((row_tiles == target)[None, :], solved, sides)
        factors.append(rows_factor)
    final_rows = keep_mask(row_tiles, panels)
    final_cols = keep_mask(col_tiles, panels)
    complement = matrix * final_rows[:, None] * final_cols[None, :]
    return (complement, jnp.concatenate(factors, axis=1), sides[0], sides[1:])


def solution(mesh):
    return jax.shard_map(
        on_device,
        mesh=mesh,
        in_specs=(P("row", "col"), P(), P("row"), P(None, "row")),
        out_specs=(P("row", "col"), P("row", None), P("row"), P(None, "row")),
        check_vma=False,
    )
```

profile of v0, /device:TPU:9, one launch (start us, length us, event | category | flops | bytes accessed | tf_op | source)
XLA Modules:
  0.0 669.9 jit_solution(17798220749902073906)
XLA Ops:
  13.4 32.9 %all-reduce.14.cloned.1.call-done = f32[256,256]{0,1:T(8,128)} async-done(((f32[256,256]{0,1:T(8,128)}), f32[256,256]{0,1:T(8,128)}) %all-reduce.14.cloned.1.call-update) | async-done | bytes 262160 | tf_op jit(solution)/shard_map/psum | solution.py:12
  46.3 1.7 broadcast_select_fusion.7
  50.8 56.7 %all-reduce.28.cloned.1.call-done = (f32[256,512]{0,1:T(8,128)}, f32[256,256]{0,1:T(8,128)}, f32[65,256]{1,0:T(8,128)}) async-done(((f32[256,512]{0,1:T(8,128)}, f32[256,256]{0,1:T(8,128)}, f32[65,256]{1,0:T(8,128)}), (f32[256,512]{0,1:T(8,128)}, f32[256,256]{0,1:T(8,128)}, f32[65,256]{1,0:T(8,128)})) %all-reduce.28.cloned.1.call-update) | async-done | bytes 853008 | tf_op jit(solution)/shard_map/psum | solution.py:12
  108.7 11.7 %cholesky.214 = f32[128,128]{1,0:T(8,128)S(1)} custom-call(f32[128,128]{1,0:T(8,128)S(1)} %cholesky.346), custom_call_target="Cholesky" | custom-call | tf_op jit(solution)/shard_map/jit(cholesky)/cholesky | solution.py:59
  120.5 9.8 %custom-call.29 = f32[1,128,128]{1,2,0:T(8,128)S(1)} custom-call(f32[1,128,128]{2,1,0:T(8,128)S(1)} %get-tuple-element.173), custom_call_target="InvertDiagBlocksLowerTriangular" | custom-call | tf_op jit(solution)/shard_map/jit(cholesky)/cholesky | solution.py:59
  130.8 11.7 %cholesky.231 = f32[128,128]{1,0:T(8,128)S(1)} custom-call(f32[128,128]{1,0:T(8,128)S(1)} %convolution_subtract_fusion.19), custom_call_target="Cholesky" | custom-call | tf_op jit(solution)/shard_map/jit(cholesky)/cholesky | solution.py:59
  144.6 4.5 while.24
  149.1 19.7 %custom-call.30 = f32[2,128,128]{1,2,0:T(8,128)S(1)} custom-call(f32[2,128,128]{2,1,0:T(8,128)S(1)} %get-tuple-element.86), custom_call_target="InvertDiagBlocksLowerTriangular" | custom-call | tf_op jit(solution)/shard_map/triangular_solve/custom-call.0 | solution.py:16
  171.7 1.8 broadcast_select_fusion.2
  176.7 31.6 %all-reduce.16.cloned.1.call-done = f32[256,256]{0,1:T(8,128)} async-done(((f32[256,256]{0,1:T(8,128)}), f32[256,256]{0,1:T(8,128)}) %all-reduce.16.cloned.1.call-update) | async-done | bytes 262160 | tf_op jit(solution)/shard_map/psum | solution.py:12
  211.2 57.8 %all-reduce.26.cloned.1.call-done = (f32[256,256]{0,1:T(8,128)}, f32[256,512]{0,1:T(8,128)}, f32[65,256]{1,0:T(8,128)}) async-done(((f32[256,256]{0,1:T(8,128)}, f32[256,512]{0,1:T(8,128)}, f32[65,256]{1,0:T(8,128)}), (f32[256,256]{0,1:T(8,128)}, f32[256,512]{0,1:T(8,128)}, f32[65,256]{1,0:T(8,128)})) %all-reduce.26.cloned.1.call-update) | async-done | bytes 853008 | tf_op jit(solution)/shard_map/psum | solution.py:12
  270.2 11.7 %cholesky.248 = f32[128,128]{1,0:T(8,128)S(1)} custom-call(f32[128,128]{1,0:T(8,128)S(1)} %cholesky.349), custom_call_target="Cholesky" | custom-call | tf_op jit(solution)/shard_map/jit(cholesky)/cholesky | solution.py:59
  282.0 9.8 %custom-call.32 = f32[1,128,128]{1,2,0:T(8,128)S(1)} custom-call(f32[1,128,128]{2,1,0:T(8,128)S(1)} %get-tuple-element.169), custom_call_target="InvertDiagBlocksLowerTriangular" | custom-call | tf_op jit(solution)/shard_map/jit(cholesky)/cholesky | solution.py:59
  292.3 11.7 %cholesky.265 = f32[128,128]{1,0:T(8,128)S(1)} custom-call(f32[128,128]{1,0:T(8,128)S(1)} %convolution_subtract_fusion.18), custom_call_target="Cholesky" | custom-call | tf_op jit(solution)/shard_map/jit(cholesky)/cholesky | solution.py:59
  306.7 4.2 while.25
  310.9 19.7 %custom-call.33 = f32[2,128,128]{1,2,0:T(8,128)S(1)} custom-call(f32[2,128,128]{2,1,0:T(8,128)S(1)} %get-tuple-element.88), custom_call_target="InvertDiagBlocksLowerTriangular" | custom-call | tf_op jit(solution)/shard_map/triangular_solve/custom-call.0 | solution.py:16
  333.1 1.8 broadcast_select_fusion.1
  338.1 31.6 %all-reduce.18.cloned.1.call-done = f32[256,256]{0,1:T(8,128)} async-done(((f32[256,256]{0,1:T(8,128)}), f32[256,256]{0,1:T(8,128)}) %all-reduce.18.cloned.1.call-update) | async-done | bytes 262160 | tf_op jit(solution)/shard_map/psum | solution.py:12
  371.4 59.4 %all-reduce.24.cloned.1.call-done = (f32[256,256]{0,1:T(8,128)}, f32[256,512]{0,1:T(8,128)}, f32[65,256]{1,0:T(8,128)}) async-done(((f32[256,256]{0,1:T(8,128)}, f32[256,512]{0,1:T(8,128)}, f32[65,256]{1,0:T(8,128)}), (f32[256,256]{0,1:T(8,128)}, f32[256,512]{0,1:T(8,128)}, f32[65,256]{1,0:T(8,128)})) %all-reduce.24.cloned.1.call-update) | async-done | bytes 853008 | tf_op jit(solution)/shard_map/psum | solution.py:12
  432.0 11.7 %cholesky.282 = f32[128,128]{1,0:T(8,128)S(1)} custom-call(f32[128,128]{1,0:T(8,128)S(1)} %cholesky.352), custom_call_target="Cholesky" | custom-call | tf_op jit(solution)/shard_map/jit(cholesky)/cholesky | solution.py:59
  443.8 9.8 %custom-call.35 = f32[1,128,128]{1,2,0:T(8,128)S(1)} custom-call(f32[1,128,128]{2,1,0:T(8,128)S(1)} %get-tuple-element.165), custom_call_target="InvertDiagBlocksLowerTriangular" | custom-call | tf_op jit(solution)/shard_map/jit(cholesky)/cholesky | solution.py:59
  454.1 11.7 %cholesky.299 = f32[128,128]{1,0:T(8,128)S(1)} custom-call(f32[128,128]{1,0:T(8,128)S(1)} %convolution_subtract_fusion.17), custom_call_target="Cholesky" | custom-call | tf_op jit(solution)/shard_map/jit(cholesky)/cholesky | solution.py:59
  468.4 4.4 while.26
  472.9 19.7 %custom-call.36 = f32[2,128,128]{1,2,0:T(8,128)S(1)} custom-call(f32[2,128,128]{2,1,0:T(8,128)S(1)} %get-tuple-element.90), custom_call_target="InvertDiagBlocksLowerTriangular" | custom-call | tf_op jit(solution)/shard_map/triangular_solve/custom-call.0 | solution.py:16
  495.1 1.8 broadcast_select_fusion
  500.1 31.6 %all-reduce.20.cloned.1.call-done = f32[256,256]{0,1:T(8,128)} async-done(((f32[256,256]{0,1:T(8,128)}), f32[256,256]{0,1:T(8,128)}) %all-reduce.20.cloned.1.call-update) | async-done | bytes 262160 | tf_op jit(solution)/shard_map/psum | solution.py:12
  533.4 59.1 %all-reduce.22.cloned.1.call-done = (f32[256,256]{0,1:T(8,128)}, f32[256,512]{0,1:T(8,128)}, f32[65,256]{1,0:T(8,128)}) async-done(((f32[256,256]{0,1:T(8,128)}, f32[256,512]{0,1:T(8,128)}, f32[65,256]{1,0:T(8,128)}), (f32[256,256]{0,1:T(8,128)}, f32[256,512]{0,1:T(8,128)}, f32[65,256]{1,0:T(8,128)})) %all-reduce.22.cloned.1.call-update) | async-done | bytes 853008 | tf_op jit(solution)/shard_map/psum | solution.py:12
  593.7 11.7 %cholesky.316 = f32[128,128]{1,0:T(8,128)S(1)} custom-call(f32[128,128]{1,0:T(8,128)S(1)} %cholesky.355), custom_call_target="Cholesky" | custom-call | tf_op jit(solution)/shard_map/jit(cholesky)/cholesky | solution.py:59
  605.5 9.8 %custom-call.38 = f32[1,128,128]{1,2,0:T(8,128)S(1)} custom-call(f32[1,128,128]{2,1,0:T(8,128)S(1)} %get-tuple-element.161), custom_call_target="InvertDiagBlocksLowerTriangular" | custom-call | tf_op jit(solution)/shard_map/jit(cholesky)/cholesky | solution.py:59
  615.8 11.7 %cholesky.333 = f32[128,128]{1,0:T(8,128)S(1)} custom-call(f32[128,128]{1,0:T(8,128)S(1)} %convolution_subtract_fusion.16), custom_call_target="Cholesky" | custom-call | tf_op jit(solution)/shard_map/jit(cholesky)/cholesky | solution.py:59
  630.2 4.2 while.27
  634.4 19.7 %custom-call.39 = f32[2,128,128]{1,2,0:T(8,128)S(1)} custom-call(f32[2,128,128]{2,1,0:T(8,128)S(1)} %get-tuple-element.92), custom_call_target="InvertDiagBlocksLowerTriangular" | custom-call | tf_op jit(solution)/shard_map/triangular_solve/custom-call.0 | solution.py:16
  (207 shorter events, 65.9 us)
Async XLA Ops:
  7.2 0.7 copy-start.17
  7.2 39.1 %all-reduce.14.cloned.1.call-start = ((), (), s32[]{:S(2)}) async-start(), calls=%async_computation | async-start | bytes 524288 | tf_op jit(solution)/shard_map/psum | solution.py:12
  11.1 0.8 copy-start.12
  11.2 96.4 %all-reduce.28.cloned.1.call-start = ((), (), s32[]{:S(2)}) async-start(), calls=%async_computation.7 | async-start | bytes 1720320 | tf_op jit(solution)/shard_map/psum | solution.py:12
  11.2 0.7 copy-start.18
  48.0 160.3 %all-reduce.16.cloned.1.call-start = ((), (), s32[]{:S(2)}) async-start(), calls=%async_computation.1 | async-start | bytes 524288 | tf_op jit(solution)/shard_map/psum | solution.py:12
  107.5 1.2 copy-start.1
  144.5 24.3 %copy-start.8 = (f32[256,512]{0,1:T(8,128)S(1)}, f32[256,512]{0,1:T(8,128)}, u32[]{:S(2)}) copy-start(f32[256,512]{0,1:T(8,128)} %get-tuple-element.147) | copy-start | bytes 1572868
  169.8 1.0 copy-start
  174.2 0.9 copy-start.13
  174.3 94.7 %all-reduce.26.cloned.1.call-start = ((), (), s32[]{:S(2)}) async-start(), calls=%async_computation.6 | async-start | bytes 1720320 | tf_op jit(solution)/shard_map/psum | solution.py:12
  209.1 160.6 %all-reduce.18.cloned.1.call-start = ((), (), s32[]{:S(2)}) async-start(), calls=%async_computation.2 | async-start | bytes 524288 | tf_op jit(solution)/shard_map/psum | solution.py:12
  269.0 1.2 copy-start.6
  306.7 23.9 %copy-start.4 = (f32[256,256]{0,1:T(8,128)S(1)}, f32[256,256]{0,1:T(8,128)}, u32[]{:S(2)}) copy-start(f32[256,256]{0,1:T(8,128)} %all-reduce.16.cloned.1.call-done) | copy-start | bytes 786436
  330.6 1.0 copy-start.11
  335.6 0.9 copy-start.15
  335.6 95.1 %all-reduce.24.cloned.1.call-start = ((), (), s32[]{:S(2)}) async-start(), calls=%async_computation.5 | async-start | bytes 1720320 | tf_op jit(solution)/shard_map/psum | solution.py:12
  370.4 161.3 %all-reduce.20.cloned.1.call-start = ((), (), s32[]{:S(2)}) async-start(), calls=%async_computation.3 | async-start | bytes 524288 | tf_op jit(solution)/shard_map/psum | solution.py:12
  430.8 1.2 copy-start.5
  468.4 24.1 %copy-start.3 = (f32[256,256]{0,1:T(8,128)S(1)}, f32[256,256]{0,1:T(8,128)}, u32[]{:S(2)}) copy-start(f32[256,256]{0,1:T(8,128)} %all-reduce.18.cloned.1.call-done) | copy-start | bytes 786436
  492.6 1.0 copy-start.10
  497.6 0.9 copy-start.14
  497.6 94.9 %all-reduce.22.cloned.1.call-start = ((), (), s32[]{:S(2)}) async-start(), calls=%async_computation.4 | async-start | bytes 1720320 | tf_op jit(solution)/shard_map/psum | solution.py:12
  592.5 1.2 copy-start.7
  630.2 23.9 %copy-start.2 = (f32[256,256]{0,1:T(8,128)S(1)}, f32[256,256]{0,1:T(8,128)}, u32[]{:S(2)}) copy-start(f32[256,256]{0,1:T(8,128)} %all-reduce.20.cloned.1.call-done) | copy-start | bytes 786436
  655.0 0.9 copy-start.16
  656.1 2.0 copy-start.9
Sparse Core Ops, SparseCore 0:
  11.3 35.0 all-reduce.13
  50.8 56.6 all-reduce.27
  174.4 33.8 all-reduce.15
  212.3 56.6 all-reduce.25
  335.8 33.8 all-reduce.17
  374.0 56.6 all-reduce.23
  497.7 33.9 all-reduce.19
  535.8 56.6 all-reduce.21
where the time goes:
time: 680 us; the launch traced here: 670 us
  waiting for transfers between devices  361 us (53%)
  other arithmetic  230 us (34%)
  local copies, waits for them, and re-layouts  31.3 us (5%)
  matrix products  23.3 us (3%)
  between operations  23.1 us (3%)
    psum x8, waiting for transfers between devices, broadcast(): return lax.psum(jnp.where(mine, value, jnp.zeros_like(value)), axis)  361 us
    another operation x27, other arithmetic, on_device(): chol_tile = jnp.linalg.cholesky(diag_tile)  138 us
    another operation x9, other arithmetic, solve_right(): lax.linalg.triangular_solve(chol_tile, values, left_side=False, lower=Tru...  78.8 us
    another operation x29, local copies, waits for them, and re-layouts, solve_right(): lax.linalg.triangular_solve(chol_tile, values, left_side=False, lower=Tru...  15.9 us
  transfers between devices with their start and end apart: 8, of which 8 were waited for; matrix products, arithmetic and copies ran while one was open for 2% of the time, Pallas kernels for 0%

commit v1 on v0

v1 whole, which is shorter than its diff:
```python
import functools

import jax
import jax.numpy as jnp
from jax import lax
from jax.experimental import pallas as pl
from jax.experimental.pallas import tpu as pltpu
from jax.sharding import PartitionSpec as P

B = 256
K = 4
STRIP = 32
GROUP = 8
LANES = 128
SIDES = 72


def split(value):
    high = value.astype(jnp.bfloat16)
    low = (value - high.astype(jnp.float32)).astype(jnp.bfloat16)
    return high, low


def product(left, right, dims=((1,), (0,))):
    one = functools.partial(
        lax.dot_general,
        dimension_numbers=(dims, ((), ())),
        preferred_element_type=jnp.float32,
    )
    return one(left[0], right[0]) + (one(left[0], right[1]) + one(left[1], right[0]))


def eliminate_strip(strip, base):
    halves = [strip[:, h * LANES : (h + 1) * LANES] for h in range(B // LANES)]
    done = [[] for _ in halves]
    lane = lax.broadcasted_iota(jnp.int32, (1, LANES), 1)
    for group in range(STRIP // GROUP):
        rows = STRIP - group * GROUP
        row = lax.broadcasted_iota(jnp.int32, (rows, 1), 0)
        first = base + group * GROUP
        home, where = first // LANES, first % LANES
        columns = [
            jnp.broadcast_to(halves[home][:, where + c : where + c + 1], (rows, LANES))
            for c in range(GROUP)
        ]
        for c in range(GROUP):
            scale = lax.rsqrt(columns[c][c : c + 1, :])
            below = row > c
            factor = jnp.where(below, columns[c] * scale, 0.0)
            for d in range(c + 1, GROUP):
                columns[d] = columns[d] - factor * (columns[d][c : c + 1, :] * scale)
            for h in range(len(halves)):
                pivot = halves[h][c : c + 1, :] * scale
                rest = halves[h]
                if h == home:
                    here = lane == where + c
                    pivot = jnp.where(here, scale, pivot)
                    rest = jnp.where(here & below, 0.0, rest)
                halves[h] = jnp.where(row == c, pivot, rest - factor * pivot)
        for h in range(len(halves)):
            done[h].append(halves[h][:GROUP])
            halves[h] = halves[h][GROUP:]
    return jnp.concatenate([jnp.concatenate(part, axis=0) for part in done], axis=1)


def invert_factor(tile_ref):
    lane = lax.broadcasted_iota(jnp.int32, (1, B), 1)
    for base in range(0, B, STRIP):
        strip = eliminate_strip(tile_ref[base : base + STRIP, :], base)
        tile_ref[base : base + STRIP, :] = strip
        after = base + STRIP
        if after < B:
            own = (lane >= base) & (lane < after)
            pivot = base + lax.broadcasted_iota(jnp.int32, (STRIP, 1), 0)
            halves = split(jnp.where(own & (lane > pivot), 0.0, strip))
            turned = split(strip[:, after:].T)
            trailing = jnp.where(own, 0.0, tile_ref[after:, :])
            tile_ref[after:, :] = trailing - product(turned, halves)
    row = lax.broadcasted_iota(jnp.int32, (B, B), 0)
    col = lax.broadcasted_iota(jnp.int32, (B, B), 1)
    return jnp.where(row >= col, tile_ref[...], 0.0)


def tile_at(index):
    return pl.ds(pl.multiple_of(index * B, B), B)


def compute_kernel(
    panels, place, among, sides_among, block, sides, complement, factor, solved, work, sides_work, tile
):
    cols_here = block.shape[1]
    col_tiles = cols_here // B
    row_tile = place[0]
    first_col = place[1]
    work[...] = among[...]
    sides_work[...] = sides_among[...]
    complement[...] = block[...]
    solved[...] = sides[...]

    def step(p, gone):
        target = panels[p]
        tile[...] = work[tile_at(p), tile_at(p)]
        inverse = split(invert_factor(tile))

        def scale_tile(c, _):
            work[tile_at(p), tile_at(c)] = product(inverse, split(work[tile_at(p), tile_at(c)]))
            return 0

        lax.fori_loop(p, K + col_tiles + 1, scale_tile, 0)
        side = product(split(sides_work[:, tile_at(p)]), inverse, ((1,), (1,)))
        side_halves = split(side)

        def update_row(q, _):
            across = work[tile_at(p), tile_at(q)]
            turned = split(across.T)

            def update_tile(c, _):
                work[tile_at(q), tile_at(c)] -= product(turned, split(work[tile_at(p), tile_at(c)]))
                return 0

            lax.fori_loop(q, K + col_tiles + 1, update_tile, 0)
            sides_work[:, tile_at(q)] -= product(side_halves, split(across))
            return 0

        lax.fori_loop(p + 1, K, update_row, 0)
        mine = work[tile_at(p), pl.ds(K * B + cols_here, B)]
        mine = mine * (1.0 - gone)
        turned = mine.T
        factor[:, tile_at(p)] = turned
        turned = split(turned)
        for c in range(col_tiles):
            part = work[tile_at(p), pl.ds((K + c) * B, B)]
            complement[:, c * B : (c + 1) * B] -= product(turned, split(part))
        rest = solved[...] - product(side_halves, split(mine))
        solved[...] = jnp.where(row_tile == target, side, rest)
        return jnp.where(row_tile == target, 1.0, gone)

    gone = lax.fori_loop(0, K, step, jnp.float32(0.0))
    for c in range(col_tiles):
        keep = 1.0 - gone
        for p in range(K):
            keep = jnp.where(panels[p] == first_col + c, 0.0, keep)
        complement[:, c * B : (c + 1) * B] *= keep


def compute(panels, place, among, sides_among, block, sides):
    rows_here, cols_here = block.shape
    vmem = pl.BlockSpec(memory_space=pltpu.VMEM)
    smem = pl.BlockSpec(memory_space=pltpu.SMEM)
    return pl.pallas_call(
        compute_kernel,
        out_shape=(
            jax.ShapeDtypeStruct((rows_here, cols_here), jnp.float32),
            jax.ShapeDtypeStruct((rows_here, K * B), jnp.float32),
            jax.ShapeDtypeStruct(sides.shape, jnp.float32),
        ),
        in_specs=[smem, smem, vmem, vmem, vmem, vmem],
        out_specs=(vmem, vmem, vmem),
        scratch_shapes=[
            pltpu.VMEM(among.shape, jnp.float32),
            pltpu.VMEM(sides_among.shape, jnp.float32),
            pltpu.VMEM((B, B), jnp.float32),
        ],
        compiler_params=pltpu.CompilerParams(vmem_limit_bytes=56 * 1024 * 1024),
        cost_estimate=pl.CostEstimate(flops=10**10, bytes_accessed=10**7, transcendentals=0),
    )(panels, place, among, sides_among, block, sides)


def gather_panels(panels, row_tile, first_col, block, sides):
    cols_here = block.shape[1]
    col_tiles = cols_here // B
    mine = (panels == row_tile).astype(jnp.float32)
    rows = lax.psum((mine[:, None, None] * block[None]).reshape(K * B, cols_here), "row")
    sides_among = lax.psum(mine[:, None, None] * sides[None], "row")
    sides_among = sides_among.transpose(1, 0, 2).reshape(SIDES, K * B)
    parts = []
    for wanted in [panels[p] for p in range(K)] + [row_tile]:
        local = wanted - first_col
        held = (local >= 0) & (local < col_tiles)
        part = lax.dynamic_slice_in_dim(rows, jnp.clip(local, 0, col_tiles - 1) * B, B, 1)
        parts.append(jnp.where(held, part, 0.0))
    spread = lax.psum(jnp.concatenate(parts, axis=1), "col")
    return jnp.concatenate([spread[:, : K * B], rows, spread[:, K * B :]], axis=1), sides_among


def on_device(covariance, panels, observed, drift_basis):
    rows_here, cols_here = covariance.shape
    row_tile = lax.axis_index("row")
    first_col = lax.axis_index("col") * (cols_here // B)
    drifts = drift_basis.shape[0]
    sides = jnp.concatenate(
        [observed[None, :], drift_basis, jnp.zeros((SIDES - 1 - drifts, rows_here), jnp.float32)], axis=0
    )
    among, sides_among = gather_panels(panels, row_tile, first_col, covariance, sides)
    place = jnp.stack([row_tile, first_col]).astype(jnp.int32)
    complement, factor, solved = compute(panels, place, among, sides_among, covariance, sides)
    return complement, factor, solved[0], solved[1 : 1 + drifts]


def solution(mesh):
    return jax.shard_map(
        on_device,
        mesh=mesh,
        in_specs=(P("row", "col"), P(), P("row"), P(None, "row")),
        out_specs=(P("row", "col"), P("row", None), P("row"), P(None, "row")),
        check_vma=False,
    )
```

time: 680 us -> 347 us (0.51)
  other arithmetic: 230 us -> 17.7 us
  waiting for transfers between devices: 361 us -> 247 us
  Pallas kernels: 0 us -> 54.1 us
  local copies, waits for them, and re-layouts: 31.3 us -> 6.91 us
  matrix products: 23.3 us -> 0 us
    another operation x36 -> x1, other arithmetic: 217 us -> 0.62 us  [on_device(): place = jnp.stack([row_tile, first_col]).astype(jnp.int32)]
    psum x8 -> x2, waiting for transfers between devices: 361 us -> 247 us  [the longest x1 186 us: gather_panels(): spread = lax.psum(jnp.concatenate(parts, axis=1), 'col')]
    pallas_call x0 -> x1, Pallas kernels: none -> 54.1 us  [compute(): pl.pallas_call(compute_kernel, out_shape=(jax.ShapeDtypeStruct((rows_here...]
    another operation x37 -> x0, local copies, waits for them, and re-layouts: 16 us -> none  [the longest x29 15.9 us: solve_right(): lax.linalg.triangular_solve(chol_tile, values, left_side=False, lower=Tru...]
    another operation x44 -> x0, matrix products: 13.9 us -> none  [the longest x24 6.32 us: solve_right(): lax.linalg.triangular_solve(chol_tile, values, left_side=False, lower=Tru...]
    dot_general x8 -> x0, matrix products: 9.39 us -> none  [the longest x4 6.43 us: outer_product(): lax.dot_general(rows_factor, cols_factor, (((1,), (0,)), ((), ())), preci...]
    unnamed x0 -> x4, other arithmetic: none -> 8.42 us
    select_n x12 -> x0, other arithmetic: 8.22 us -> none  [the longest x10 8.2 us: broadcast(): return lax.psum(jnp.where(mine, value, jnp.zeros_like(value)), axis)]
  transfers between devices with their start and end apart: 8 -> 2, of which waited for: 8 -> 2; matrix products, arithmetic and copies ran while one was open for 2% -> 0% of each run, Pallas kernels for 0% -> 0%
where the time goes in v1:
time: 347 us; the launch traced here: 343 us
  waiting for transfers between devices  247 us (71%)
  Pallas kernels  54.1 us (16%)
  other arithmetic  17.7 us (5%)
  between operations  16.7 us (5%)
  local copies, waits for them, and re-layouts  6.91 us (2%)
    psum x1, waiting for transfers between devices, gather_panels(): spread = lax.psum(jnp.concatenate(parts, axis=1), 'col')  186 us
    psum x1, waiting for transfers between devices, gather_panels(): lax.psum((mine[:, None, None] * block[None]).reshape(K * B, cols_here), '...  60.9 us
    pallas_call x1, Pallas kernels, compute(): pl.pallas_call(compute_kernel, out_shape=(jax.ShapeDtypeStruct((rows_here...  54.1 us
    unnamed x4, other arithmetic  8.42 us
  transfers between devices with their start and end apart: 2, of which 2 were waited for; matrix products, arithmetic and copies ran while one was open for 0% of the time, Pallas kernels for 0%

profile of v1, /device:TPU:9, one launch (start us, length us, event | category | flops | bytes accessed | tf_op | source)
XLA Modules:
  0.0 342.9 jit_solution(15703949824474139462)
XLA Ops:
  7.2 0.0 copy-start.2
  7.2 0.0 all-reduce.6.cloned.1.call-start
  7.2 0.7 compare_convert_fusion
  7.9 0.1 broadcast_bitcast_fusion
  8.0 0.1 pad.2.clone
  8.1 0.9 maximum_maximum_fusion.sides
  9.0 0.0 copy-start.1
  9.0 0.1 broadcast_multiply_fusion
  9.1 0.8 copy.9
  9.9 2.6 bitcast_multiply_fusion
  12.5 0.0 all-reduce.6.cloned.1.call-update
  12.5 0.0 all-reduce.4.cloned.1.call-start
  12.6 0.0 copy-done.2
  12.6 0.7 fusion
  15.9 60.9 %all-reduce.6.cloned.1.call-done = (f32[1024,512]{1,0:T(8,128)}, f32[72,1024]{1,0:T(8,128)}) async-done(((f32[1024,512]{1,0:T(8,128)}, f32[72,1024]{1,0:T(8,128)}), (f32[1024,512]{1,0:T(8,128)}, f32[72,1024]{1,0:T(8,128)})) %all-reduce.6.cloned.1.call-update) | async-done | bytes 2392080 | tf_op jit(solution)/shard_map/psum | solution.py:173
  76.8 0.0 copy-start
  76.8 2.5 select_dynamic-update-slice_fusion.4
  79.3 2.5 select_dynamic-update-slice_fusion.3
  81.7 2.3 select_dynamic-update-slice_fusion.2
  84.0 0.0 copy-done.1
  84.0 0.0 copy-done
  84.0 1.2 select_dynamic-update-slice_fusion.1
  85.2 1.2 select_dynamic-update-slice_fusion
  86.4 0.0 all-reduce.4.cloned.1.call-update
  86.4 0.6 pad_add_fusion.place
  87.0 186.4 %all-reduce.4.cloned.1.call-done = f32[1024,1280]{1,0:T(8,128)} async-done(((f32[1024,1280]{1,0:T(8,128)}), f32[1024,1280]{1,0:T(8,128)}) %all-reduce.4.cloned.1.call-update) | async-done | bytes 5242896 | tf_op jit(solution)/shard_map/psum | solution.py:182
  273.4 1.2 slice-done
  274.6 1.3 slice-done.1
  275.9 3.2 pad_maximum_fusion.among
  279.1 54.1 %shard_map.75 = (f32[256,512]{1,0:T(8,128)}, f32[256,1024]{1,0:T(8,128)}, f32[72,256]{1,0:T(8,128)}) custom-call(s32[4]{0:T(128)} %panels.1, s32[2]{0:T(128)} %pad_add_fusion.place, f32[1024,1792]{1,0:T(8,128)} %pad_maximum_fusion.among, f32[72,1024]{1,0:T(8,128)} %get-tuple-element.11.sides_among, f32[256,512]{1,0:T(8,128)} %block.1, f32[72,256]{1,0:T(8,128)} %copy-done.1), custom_call_target="tpu_custom_call" | custom-call | flops 10000000000 | bytes 10000000 | tf_op jit(solution)/shard_map/pallas_call | solution.py:150
  333.2 1.3 slice.30
  334.5 1.5 slice.31
  (4 shorter events, 0.0 us)
Async XLA Ops:
  7.2 5.4 %copy-start.2 = (s32[4]{0:T(128)S(1)}, s32[4]{0:T(128)}, u32[]{:S(2)}) copy-start(s32[4]{0:T(128)} %panels.1) | copy-start | bytes 52
  7.2 69.6 %all-reduce.6.cloned.1.call-start = ((), (), s32[]{:S(2)}) async-start(), calls=%async_computation.1 | async-start | bytes 4784128 | tf_op jit(solution)/shard_map/psum | solution.py:173
  9.0 75.0 %copy-start.1 = (f32[72,256]{1,0:T(8,128)}, f32[72,256]{1,0:T(8,128)S(1)}, u32[]{:S(2)}) copy-start(f32[72,256]{1,0:T(8,128)S(1)} %maximum_maximum_fusion.sides) | copy-start | bytes 221188
  12.5 260.9 %all-reduce.4.cloned.1.call-start = ((), (), s32[]{:S(2)}) async-start(), calls=%async_computation | async-start | bytes 10485760 | tf_op jit(solution)/shard_map/psum | solution.py:182
  76.8 7.2 %copy-start = (f32[1024,512]{1,0:T(8,128)S(1)}, f32[1024,512]{1,0:T(8,128)}, u32[]{:S(2)}) copy-start(f32[1024,512]{1,0:T(8,128)} %get-tuple-element.10) | copy-start | bytes 6291460
  273.4 1.2 slice-start
  273.4 2.5 slice-start.1
Sparse Core Ops, SparseCore 0:
  12.6 64.1 all-reduce.5
  86.5 186.8 all-reduce.3

commit v2 on v1

--- a/solution.py
+++ b/solution.py
@@ -12,7 +12,9 @@
 STRIP = 32
 GROUP = 8
 LANES = 128
-SIDES = 72
+SIDES = 128
+SHARES = 8
+SHARE = B // SHARES
 
 
 def split(value):
@@ -85,17 +87,21 @@
     return pl.ds(pl.multiple_of(index * B, B), B)
 
 
-def compute_kernel(
-    panels, place, among, sides_among, block, sides, complement, factor, solved, work, sides_work, tile
-):
-    cols_here = block.shape[1]
+def compute_kernel(panels, place, among_panels, among_cols, among_rows, block, complement, factor, solved, work, total, tile):
+    cols_here = complement.shape[1]
     col_tiles = cols_here // B
+    tiles = K + col_tiles + 1
     row_tile = place[0]
     first_col = place[1]
-    work[...] = among[...]
-    sides_work[...] = sides_among[...]
-    complement[...] = block[...]
-    solved[...] = sides[...]
+    for p in range(K):
+        for k in range(SHARES):
+            rows = slice(p * B + k * SHARE, p * B + (k + 1) * SHARE)
+            work[rows, p * B : K * B] = among_panels[k, p, :, p * B :]
+            work[rows, K * B : K * B + cols_here] = among_cols[k, p, :, :cols_here]
+            work[rows, K * B + cols_here : tiles * B] = among_rows[k, p]
+            work[rows, tiles * B :] = among_cols[k, p, :, cols_here:]
+    total[...] = block[...]
+    tail = pl.ds(tiles * B, SIDES)
 
     def step(p, gone):
         target = panels[p]
@@ -106,33 +112,30 @@
             work[tile_at(p), tile_at(c)] = product(inverse, split(work[tile_at(p), tile_at(c)]))
             return 0
 
-        lax.fori_loop(p, K + col_tiles + 1, scale_tile, 0)
-        side = product(split(sides_work[:, tile_at(p)]), inverse, ((1,), (1,)))
+        lax.fori_loop(p + 1, tiles, scale_tile, 0)
+        side = product(inverse, split(work[tile_at(p), tail]))
         side_halves = split(side)
 
         def update_row(q, _):
-            across = work[tile_at(p), tile_at(q)]
-            turned = split(across.T)
+            turned = split(work[tile_at(p), tile_at(q)].T)
 
             def update_tile(c, _):
                 work[tile_at(q), tile_at(c)] -= product(turned, split(work[tile_at(p), tile_at(c)]))
                 return 0
 
-            lax.fori_loop(q, K + col_tiles + 1, update_tile, 0)
-            sides_work[:, tile_at(q)] -= product(side_halves, split(across))
+            lax.fori_loop(q, tiles, update_tile, 0)
+            work[tile_at(q), tail] -= product(turned, side_halves)
             return 0
 
         lax.fori_loop(p + 1, K, update_row, 0)
-        mine = work[tile_at(p), pl.ds(K * B + cols_here, B)]
-        mine = mine * (1.0 - gone)
-        turned = mine.T
-        factor[:, tile_at(p)] = turned
-        turned = split(turned)
+        mine = work[tile_at(p), pl.ds((tiles - 1) * B, B)].T * (1.0 - gone)
+        factor[:, tile_at(p)] = mine
+        turned = split(mine)
         for c in range(col_tiles):
             part = work[tile_at(p), pl.ds((K + c) * B, B)]
-            complement[:, c * B : (c + 1) * B] -= product(turned, split(part))
-        rest = solved[...] - product(side_halves, split(mine))
-        solved[...] = jnp.where(row_tile == target, side, rest)
+            total[:, c * B : (c + 1) * B] -= product(turned, split(part))
+        rest = total[:, cols_here:] - product(turned, side_halves)
+        total[:, cols_here:] = jnp.where(row_tile == target, side, rest)
         return jnp.where(row_tile == target, 1.0, gone)
 
     gone = lax.fori_loop(0, K, step, jnp.float32(0.0))
@@ -140,11 +143,12 @@
         keep = 1.0 - gone
         for p in range(K):
             keep = jnp.where(panels[p] == first_col + c, 0.0, keep)
-        complement[:, c * B : (c + 1) * B] *= keep
-
-
-def compute(panels, place, among, sides_among, block, sides):
-    rows_here, cols_here = block.shape
+        complement[:, c * B : (c + 1) * B] = total[:, c * B : (c + 1) * B] * keep
+    solved[...] = total[:, cols_here:].T
+
+
+def compute(panels, place, shares, block):
+    rows_here, cols_here = block.shape[0], block.shape[1] - SIDES
     vmem = pl.BlockSpec(memory_space=pltpu.VMEM)
     smem = pl.BlockSpec(memory_space=pltpu.SMEM)
     return pl.pallas_call(
@@ -152,27 +156,147 @@
         out_shape=(
             jax.ShapeDtypeStruct((rows_here, cols_here), jnp.float32),
             jax.ShapeDtypeStruct((rows_here, K * B), jnp.float32),
-            jax.ShapeDtypeStruct(sides.shape, jnp.float32),
+            jax.ShapeDtypeStruct((SIDES, rows_here), jnp.float32),
         ),
         in_specs=[smem, smem, vmem, vmem, vmem, vmem],
         out_specs=(vmem, vmem, vmem),
         scratch_shapes=[
-            pltpu.VMEM(among.shape, jnp.float32),
-            pltpu.VMEM(sides_among.shape, jnp.float32),
+            pltpu.VMEM((K * B, K * B + cols_here + B + SIDES), jnp.float32),
+            pltpu.VMEM(block.shape, jnp.float32),
             pltpu.VMEM((B, B), jnp.float32),
         ],
         compiler_params=pltpu.CompilerParams(vmem_limit_bytes=56 * 1024 * 1024),
         cost_estimate=pl.CostEstimate(flops=10**10, bytes_accessed=10**7, transcendentals=0),
-    )(panels, place, among, sides_among, block, sides)
-
-
-def gather_panels(panels, row_tile, first_col, block, sides):
-    cols_here = block.shape[1]
+    )(panels, place, *shares, block)
+
+
+def gather_kernel(
+    panels, block, among_panels, among_cols, among_rows, pieces, slabs,
+    piece_send, piece_recv, slab_send, slab_recv, col_send, col_recv, colf_send, colf_recv,
+    row_send, row_recv, pan_send, pan_recv, panf_send, panf_recv,
+):
+    me = lax.axis_index("row")
+    layer = lax.axis_index("col")
+    layers = slabs.shape[0] // 2
+    chips = SHARES // 2
+    chip = me // 2
+    core = me % 2
+    other = chip * 2 + (1 - core)
+    cols_here = block.shape[1] - SIDES
+
+    barrier = pltpu.get_barrier_semaphore()
+    for o in range(1, SHARES):
+        pl.semaphore_signal(barrier, inc=1, device_id={"row": (me + o) % SHARES}, device_id_type=pl.DeviceIdType.MESH)
+    for o in range(1, layers):
+        pl.semaphore_signal(barrier, inc=1, device_id={"col": (layer + o) % layers}, device_id_type=pl.DeviceIdType.MESH)
+    pl.semaphore_wait(barrier, SHARES - 1 + layers - 1)
+
+    def send(source, target, sends, recvs, where):
+        copy = pltpu.make_async_remote_copy(
+            src_ref=source, dst_ref=target, send_sem=sends, recv_sem=recvs,
+            device_id=where, device_id_type=pl.DeviceIdType.MESH,
+        )
+        copy.start()
+        return copy
+
+    def share_of(index):
+        return pl.ds(pl.multiple_of(index * SHARE, SHARE), SHARE)
+
+    dealt = []
+    for o in range(1, SHARES):
+        peer = (me + o) % SHARES
+        dealt.append(
+            send(block.at[share_of(peer)], pieces.at[me], piece_send.at[o], piece_recv.at[o], {"row": peer})
+        )
+    pieces[me] = block[share_of(me), :]
+    for copy in dealt:
+        copy.wait_recv()
+
+    for s in range(K):
+        packed = pieces[panels[s]]
+        among_cols[me, s] = packed
+        for c in range(2):
+            slabs[2 * layer + c, s] = packed[:, c * B : (c + 1) * B]
+    mine = slabs.at[pl.ds(2 * layer, 2)]
+    spread = [
+        send(mine, mine, slab_send.at[o], slab_recv.at[o], {"col": (layer + o) % layers})
+        for o in range(1, layers)
+    ]
+    col_share = among_cols.at[me]
+    cols = [
+        send(col_share, col_share, col_send.at[o], col_recv.at[o], {"row": ((chip + o) % chips) * 2 + core})
+        for o in range(1, chips)
+    ]
+    passed = [send(col_share, col_share, colf_send.at[0], colf_recv.at[0], {"row": other})]
+    for copy in spread:
+        copy.wait_recv()
+
+    for s in range(K):
+        for q in range(s, K):
+            among_panels[me, s, :, q * B : (q + 1) * B] = slabs[panels[q], s]
+    pans = []
+    for o in range(1, chips):
+        for s in range(K):
+            part = among_panels.at[me, s, :, pl.ds(s * B, (K - s) * B)]
+            pans.append(
+                send(part, part, pan_send.at[o, s], pan_recv.at[o, s], {"row": ((chip + o) % chips) * 2 + core})
+            )
+    for s in range(K):
+        part = among_panels.at[me, s, :, pl.ds(s * B, (K - s) * B)]
+        passed.append(send(part, part, panf_send.at[0, s], panf_recv.at[0, s], {"row": other}))
+    rows = []
+    for o in range(1, SHARES):
+        peer = (me + o) % SHARES
+        rows.append(send(slabs.at[peer], among_rows.at[me], row_send.at[o], row_recv.at[o], {"row": peer}))
+    among_rows[me] = slabs[me]
+
+    for o in range(1, chips):
+        cols[o - 1].wait_recv()
+        share = among_cols.at[((chip + chips - o) % chips) * 2 + core]
+        passed.append(send(share, share, colf_send.at[o], colf_recv.at[o], {"row": other}))
+    for o in range(1, chips):
+        for s in range(K):
+            pans[(o - 1) * K + s].wait_recv()
+            part = among_panels.at[((chip + chips - o) % chips) * 2 + core, s, :, pl.ds(s * B, (K - s) * B)]
+            passed.append(send(part, part, panf_send.at[o, s], panf_recv.at[o, s], {"row": other}))
+    for copy in passed + rows:
+        copy.wait_recv()
+    for copy in dealt + spread + cols + pans + rows + passed:
+        copy.wait_send()
+
+
+def gather_by_copies(panels, block, layers):
+    cols_here = block.shape[1] - SIDES
+    vmem = pl.BlockSpec(memory_space=pltpu.VMEM)
+    smem = pl.BlockSpec(memory_space=pltpu.SMEM)
+    chips = SHARES // 2
+    dma = pltpu.SemaphoreType.DMA
+    return pl.pallas_call(
+        gather_kernel,
+        out_shape=(
+            jax.ShapeDtypeStruct((SHARES, K, SHARE, K * B), jnp.float32),
+            jax.ShapeDtypeStruct((SHARES, K, SHARE, cols_here + SIDES), jnp.float32),
+            jax.ShapeDtypeStruct((SHARES, K, SHARE, B), jnp.float32),
+        ),
+        in_specs=[smem, vmem],
+        out_specs=(vmem, vmem, vmem),
+        scratch_shapes=[
+            pltpu.VMEM((SHARES, SHARE, cols_here + SIDES), jnp.float32),
+            pltpu.VMEM((2 * layers, K, SHARE, B), jnp.float32),
+        ]
+        + [dma((SHARES,))] * 2 + [dma((layers,))] * 2 + [dma((chips,))] * 4
+        + [dma((SHARES,))] * 2 + [dma((chips, K))] * 4,
+        compiler_params=pltpu.CompilerParams(
+            collective_id=0, has_side_effects=True, vmem_limit_bytes=56 * 1024 * 1024
+        ),
+    )(panels, block)
+
+
+def gather_by_sums(panels, row_tile, first_col, block):
+    cols_here = block.shape[1] - SIDES
     col_tiles = cols_here // B
     mine = (panels == row_tile).astype(jnp.float32)
-    rows = lax.psum((mine[:, None, None] * block[None]).reshape(K * B, cols_here), "row")
-    sides_among = lax.psum(mine[:, None, None] * sides[None], "row")
-    sides_among = sides_among.transpose(1, 0, 2).reshape(SIDES, K * B)
+    rows = lax.psum((mine[:, None, None] * block[None]).reshape(K * B, -1), "row")
     parts = []
     for wanted in [panels[p] for p in range(K)] + [row_tile]:
         local = wanted - first_col
@@ -180,10 +304,13 @@
         part = lax.dynamic_slice_in_dim(rows, jnp.clip(local, 0, col_tiles - 1) * B, B, 1)
         parts.append(jnp.where(held, part, 0.0))
     spread = lax.psum(jnp.concatenate(parts, axis=1), "col")
-    return jnp.concatenate([spread[:, : K * B], rows, spread[:, K * B :]], axis=1), sides_among
-
-
-def on_device(covariance, panels, observed, drift_basis):
+    return [
+        part.reshape(K, SHARES, SHARE, -1).transpose(1, 0, 2, 3)
+        for part in (spread[:, : K * B], rows, spread[:, K * B :])
+    ]
+
+
+def on_device(paired, layers, covariance, panels, observed, drift_basis):
     rows_here, cols_here = covariance.shape
     row_tile = lax.axis_index("row")
     first_col = lax.axis_index("col") * (cols_here // B)
@@ -191,15 +318,21 @@
     sides = jnp.concatenate(
         [observed[None, :], drift_basis, jnp.zeros((SIDES - 1 - drifts, rows_here), jnp.float32)], axis=0
     )
-    among, sides_among = gather_panels(panels, row_tile, first_col, covariance, sides)
+    block = jnp.concatenate([covariance, sides.T], axis=1)
+    if paired:
+        shares = gather_by_copies(panels, block, layers)
+    else:
+        shares = gather_by_sums(panels, row_tile, first_col, block)
     place = jnp.stack([row_tile, first_col]).astype(jnp.int32)
-    complement, factor, solved = compute(panels, place, among, sides_among, covariance, sides)
+    complement, factor, solved = compute(panels, place, shares, block)
     return complement, factor, solved[0], solved[1 : 1 + drifts]
 
 
 def solution(mesh):
+    row, col = mesh.shape["row"], mesh.shape["col"]
+    paired = row == SHARES and 2 * col == row
     return jax.shard_map(
-        on_device,
+        functools.partial(on_device, paired, col),
         mesh=mesh,
         in_specs=(P("row", "col"), P(), P("row"), P(None, "row")),
         out_specs=(P("row", "col"), P("row", None), P("row"), P(None, "row")),

time: 347 us -> 130 us (0.37); the launches traced: 343 us -> 130 us
  waiting for transfers between devices: 247 us -> 0 us
  Pallas kernels: 54.1 us -> 122 us
  between operations: 16.7 us -> 0.67 us
  other arithmetic: 17.7 us -> 2.69 us
    psum x2 -> x0, waiting for transfers between devices: 247 us -> none  [the longest x1 186 us: gather_panels(): spread = lax.psum(jnp.concatenate(parts, axis=1), 'col')]
    pallas_call x0 -> x1, Pallas kernels: none -> 68.5 us  [gather_by_copies(): pl.pallas_call(gather_kernel, out_shape=(jax.ShapeDtypeStruct((SHARES, K,...]
    unnamed x4 -> x0, other arithmetic: 8.42 us -> none
  transfers between devices with their start and end apart: 2 -> 0, of which waited for: 2 -> 0; matrix products, arithmetic and copies ran while one was open for 0% -> 0% of each run, Pallas kernels for 0% -> 0%
where the time goes in v2:
time: 130 us
  Pallas kernels  122 us (94%)
  local copies, waits for them, and re-layouts  4.6 us (4%)
  other arithmetic  2.69 us (2%)
    pallas_call x1, Pallas kernels, gather_by_copies(): pl.pallas_call(gather_kernel, out_shape=(jax.ShapeDtypeStruct((SHARES, K,...  68.5 us
    pallas_call x1, Pallas kernels, compute(): pl.pallas_call(compute_kernel, out_shape=(jax.ShapeDtypeStruct((rows_here...  53.4 us
    slice x2, local copies, waits for them, and re-layouts, on_device(): return (complement, factor, solved[0], solved[1:1 + drifts])  2.78 us

profile of v2, /device:TPU:9, one launch (start us, length us, event | category | flops | bytes accessed | tf_op | source)
XLA Modules:
  0.0 129.8 jit_solution(3915527686547996834)
XLA Ops:
  0.6 0.6 pad_add_fusion.place
  1.2 0.1 pad.4.clone
  1.3 0.8 copy.9
  2.1 0.9 copy.10
  3.1 0.1 maximum_bitcast_fusion
  3.2 2.0 %pad_maximum_fusion.block = f32[256,640]{1,0:T(8,128)} fusion(f32[256,128]{1,0:T(8,128)S(1)} %maximum_bitcast_fusion, f32[256,512]{1,0:T(8,128)} %param.4), kind=kLoop, calls=%fused_computation | loop fusion | flops 163840 | bytes 1310720 | tf_op jit(solution)/shard_map/concatenate | solution.py:321
  5.2 68.5 %shard_map.75 = (f32[8,4,32,1024]{3,2,1,0:T(8,128)}, f32[8,4,32,640]{3,2,1,0:T(8,128)}, f32[8,4,32,256]{3,2,1,0:T(8,128)}) custom-call(s32[4]{0:T(128)} %panels.3, f32[256,640]{1,0:T(8,128)} %pad_maximum_fusion.block), custom_call_target="tpu_custom_call" | custom-call | tf_op jit(solution)/shard_map/pallas_call | solution.py:274
  73.7 53.4 %shard_map.76 = (f32[256,512]{1,0:T(8,128)}, f32[256,1024]{1,0:T(8,128)}, f32[128,256]{1,0:T(8,128)}) custom-call(s32[4]{0:T(128)} %panels.3, s32[2]{0:T(128)} %pad_add_fusion.place, f32[8,4,32,1024]{3,2,1,0:T(8,128)} %get-tuple-element.10.among_panels, f32[8,4,32,640]{3,2,1,0:T(8,128)} %get-tuple-element.11.among_cols, ...), custom_call_target="tpu_custom_call" | custom-call | flops 10000000000 | bytes 10000000 | tf_op jit(solution)/shard_map/pallas_call | solution.py:154
  127.0 1.3 slice.6
  128.3 1.5 %slice.7 = f32[64,256]{1,0:T(8,128)} slice(f32[128,256]{1,0:T(8,128)} %get-tuple-element.15), slice={[1:65], [0:256]} | slice | bytes 131072 | tf_op jit(solution)/shard_map/slice | solution.py:328
  (1 shorter events, 0.0 us)

commit v3 on v1

v3 whole, which is shorter than its diff:
```python
import functools

import jax
import jax.numpy as jnp
from jax import lax
from jax.experimental import pallas as pl
from jax.experimental.pallas import tpu as pltpu
from jax.sharding import PartitionSpec as P

B = 256
K = 4
STRIP = 32
GROUP = 8
LANES = 128
SIDES = 128
SHARES = 8
SHARE = B // SHARES
PARTS = ((0, 1), (1, K))


def split(value):
    high = value.astype(jnp.bfloat16)
    low = (value - high.astype(jnp.float32)).astype(jnp.bfloat16)
    return high, low


def product(left, right, dims=((1,), (0,))):
    one = functools.partial(
        lax.dot_general,
        dimension_numbers=(dims, ((), ())),
        preferred_element_type=jnp.float32,
    )
    return one(left[0], right[0]) + (one(left[0], right[1]) + one(left[1], right[0]))


def eliminate_strip(strip, base):
    halves = [strip[:, h * LANES : (h + 1) * LANES] for h in range(B // LANES)]
    done = [[] for _ in halves]
    lane = lax.broadcasted_iota(jnp.int32, (1, LANES), 1)
    for group in range(STRIP // GROUP):
        rows = STRIP - group * GROUP
        row = lax.broadcasted_iota(jnp.int32, (rows, 1), 0)
        first = base + group * GROUP
        home, where = first // LANES, first % LANES
        columns = [
            jnp.broadcast_to(halves[home][:, where + c : where + c + 1], (rows, LANES))
            for c in range(GROUP)
        ]
        for c in range(GROUP):
            scale = lax.rsqrt(columns[c][c : c + 1, :])
            below = row > c
            factor = jnp.where(below, columns[c] * scale, 0.0)
            for d in range(c + 1, GROUP):
                columns[d] = columns[d] - factor * (columns[d][c : c + 1, :] * scale)
            for h in range(len(halves)):
                pivot = halves[h][c : c + 1, :] * scale
                rest = halves[h]
                if h == home:
                    here = lane == where + c
                    pivot = jnp.where(here, scale, pivot)
                    rest = jnp.where(here & below, 0.0, rest)
                halves[h] = jnp.where(row == c, pivot, rest - factor * pivot)
        for h in range(len(halves)):
            done[h].append(halves[h][:GROUP])
            halves[h] = halves[h][GROUP:]
    return jnp.concatenate([jnp.concatenate(part, axis=0) for part in done], axis=1)


def invert_factor(tile_ref, halfway):
    lane = lax.broadcasted_iota(jnp.int32, (1, B), 1)
    for base in range(0, B, STRIP):
        if base == B // 2:
            halfway()
        strip = eliminate_strip(tile_ref[base : base + STRIP, :], base)
        tile_ref[base : base + STRIP, :] = strip
        after = base + STRIP
        if after < B:
            own = (lane >= base) & (lane < after)
            pivot = base + lax.broadcasted_iota(jnp.int32, (STRIP, 1), 0)
            halves = split(jnp.where(own & (lane > pivot), 0.0, strip))
            turned = split(strip[:, after:].T)
            trailing = jnp.where(own, 0.0, tile_ref[after:, :])
            tile_ref[after:, :] = trailing - product(turned, halves)
    row = lax.broadcasted_iota(jnp.int32, (B, B), 0)
    col = lax.broadcasted_iota(jnp.int32, (B, B), 1)
    return jnp.where(row >= col, tile_ref[...], 0.0)


def tile_at(index):
    return pl.ds(pl.multiple_of(index * B, B), B)


def run_steps(panels, shares, outs, work, total, tile, halfway, arrived):
    among_panels, among_cols, among_rows = shares
    complement, factor, data, drift = outs
    cols_here = complement.shape[1]
    drifts = drift.shape[0]
    col_tiles = cols_here // B
    tiles = K + col_tiles + 1
    row_tile = lax.axis_index("row")
    first_col = lax.axis_index("col") * col_tiles
    tail = pl.ds(tiles * B, SIDES)
    tile[...] = among_panels[:, 0, :, :B].reshape(B, B)

    def at_first(p, action):
        def run():
            pl.when(p == 0)(action)

        return run

    def assemble():
        arrived()
        for p in range(K):
            for k in range(SHARES):
                rows = slice(p * B + k * SHARE, p * B + (k + 1) * SHARE)
                work[rows, p * B : K * B] = among_panels[k, p, :, p * B :]
                work[rows, K * B : K * B + cols_here] = among_cols[k, p, :, :cols_here]
                work[rows, K * B + cols_here : tiles * B] = among_rows[k, p]
                work[rows, tiles * B :] = among_cols[k, p, :, cols_here:]

    def step(p, gone):
        target = panels[p]
        inverse = split(invert_factor(tile, at_first(p, halfway)))
        at_first(p, assemble)()

        def scale_tile(c, _):
            work[tile_at(p), tile_at(c)] = product(inverse, split(work[tile_at(p), tile_at(c)]))
            return 0

        lax.fori_loop(p + 1, tiles, scale_tile, 0)
        side = product(inverse, split(work[tile_at(p), tail]))
        side_halves = split(side)

        def update_row(q, _):
            turned = split(work[tile_at(p), tile_at(q)].T)

            def update_tile(c, _):
                work[tile_at(q), tile_at(c)] -= product(turned, split(work[tile_at(p), tile_at(c)]))
                return 0

            lax.fori_loop(q, tiles, update_tile, 0)
            work[tile_at(q), tail] -= product(turned, side_halves)
            return 0

        lax.fori_loop(p + 1, K, update_row, 0)
        mine = work[tile_at(p), pl.ds((tiles - 1) * B, B)].T * (1.0 - gone)
        factor[:, tile_at(p)] = mine
        turned = split(mine)
        for c in range(col_tiles):
            part = work[tile_at(p), pl.ds((K + c) * B, B)]
            total[:, c * B : (c + 1) * B] -= product(turned, split(part))
        rest = total[:, cols_here:] - product(turned, side_halves)
        total[:, cols_here:] = jnp.where(row_tile == target, side, rest)
        following = jnp.minimum(p + 1, K - 1)
        tile[...] = work[tile_at(following), tile_at(following)]
        return jnp.where(row_tile == target, 1.0, gone)

    gone = lax.fori_loop(0, K, step, jnp.float32(0.0))
    for c in range(col_tiles):
        keep = 1.0 - gone
        for p in range(K):
            keep = jnp.where(panels[p] == first_col + c, 0.0, keep)
        complement[:, c * B : (c + 1) * B] = total[:, c * B : (c + 1) * B] * keep
    solved = total[:, cols_here:].T
    drift[...] = solved[:drifts]
    data[...] = solved[drifts : drifts + 1]


def stack_block(covariance, data, drift, total):
    cols_here = covariance.shape[1]
    filler = jnp.zeros((SIDES - drift.shape[0] - 1, B), jnp.float32)
    total[:, :cols_here] = covariance[...]
    total[:, cols_here:] = jnp.concatenate([drift[...], data[...], filler], axis=0).T


def local_kernel(panels, covariance, data, drift, *refs):
    shares, outs, (work, total, tile) = refs[:3], refs[3:7], refs[7:]
    stack_block(covariance, data, drift, total)
    run_steps(panels, shares, outs, work, total, tile, lambda: None, lambda: None)


def copies_kernel(panels, covariance, data, drift, *refs):
    outs, (work, total, tile), shares, (pieces, *slabs) = refs[:4], refs[4:7], refs[7:10], refs[10:13]
    (
        piece_send, piece_recv, slab_send, slab_recv, col_send, col_recv, colf_send, colf_recv,
        row_send, row_recv, pan_send, pan_recv, panf_send, panf_recv,
    ) = refs[13:]
    among_panels, among_cols, among_rows = shares
    me = lax.axis_index("row")
    layer = lax.axis_index("col")
    layers = slabs[0].shape[0] // 2
    chips = SHARES // 2
    chip = me // 2
    core = me % 2
    other = chip * 2 + (1 - core)

    barrier = pltpu.get_barrier_semaphore()
    for o in range(1, SHARES):
        pl.semaphore_signal(barrier, inc=1, device_id={"row": (me + o) % SHARES}, device_id_type=pl.DeviceIdType.MESH)
    for o in range(1, layers):
        pl.semaphore_signal(barrier, inc=1, device_id={"col": (layer + o) % layers}, device_id_type=pl.DeviceIdType.MESH)
    pl.semaphore_wait(barrier, SHARES - 1 + layers - 1)

    stack_block(covariance, data, drift, total)

    def send(source, target, sends, recvs, where):
        copy = pltpu.make_async_remote_copy(
            src_ref=source, dst_ref=target, send_sem=sends, recv_sem=recvs,
            device_id=where, device_id_type=pl.DeviceIdType.MESH,
        )
        copy.start()
        return copy

    def share_of(index):
        return pl.ds(pl.multiple_of(index * SHARE, SHARE), SHARE)

    def twin(o):
        return {"row": ((chip + o) % chips) * 2 + core}

    def twin_share(o):
        return ((chip + chips - o) % chips) * 2 + core

    def panel_part(share, s):
        return among_panels.at[share, s, :, pl.ds(s * B, (K - s) * B)]

    dealt = []
    for o in range(1, SHARES):
        peer = (me + o) % SHARES
        dealt.append(
            send(total.at[share_of(peer)], pieces.at[me], piece_send.at[o], piece_recv.at[o], {"row": peer})
        )
    pieces[me] = total[share_of(me), :]
    for copy in dealt:
        copy.wait_recv()

    spread = []
    for part, (low, high) in enumerate(PARTS):
        for s in range(low, high):
            packed = pieces[panels[s]]
            among_cols[me, s] = packed
            for c in range(2):
                slabs[part][2 * layer + c, s - low] = packed[:, c * B : (c + 1) * B]
        mine = slabs[part].at[pl.ds(2 * layer, 2)]
        spread.append([
            send(mine, mine, slab_send.at[o, part], slab_recv.at[o, part], {"col": (layer + o) % layers})
            for o in range(1, layers)
        ])
    col_share = among_cols.at[me]
    cols = [send(col_share, col_share, col_send.at[o], col_recv.at[o], twin(o)) for o in range(1, chips)]
    passed = [send(col_share, col_share, colf_send.at[0], colf_recv.at[0], {"row": other})]

    pans, firsts, laters = [], [], []
    for s in range(K):
        for part, (low, high) in enumerate(PARTS):
            if s == low:
                for copy in spread[part]:
                    copy.wait_recv()
            if low <= s < high:
                for q in range(s, K):
                    among_panels[me, s, :, q * B : (q + 1) * B] = slabs[part][panels[q], s - low]
        part = panel_part(me, s)
        pans.append([send(part, part, pan_send.at[o, s], pan_recv.at[o, s], twin(o)) for o in range(1, chips)])
        (laters if s else firsts).append(send(part, part, panf_send.at[0, s], panf_recv.at[0, s], {"row": other}))
    rows = []
    for o in range(1, SHARES):
        peer = (me + o) % SHARES
        for part, (low, high) in enumerate(PARTS):
            source = slabs[part].at[peer]
            target = among_rows.at[me, pl.ds(low, high - low)]
            rows.append(send(source, target, row_send.at[o, part], row_recv.at[o, part], {"row": peer}))
    for part, (low, high) in enumerate(PARTS):
        among_rows[me, low:high] = slabs[part][me]

    def pass_panels(o, s):
        pans[s][o - 1].wait_recv()
        part = panel_part(twin_share(o), s)
        return send(part, part, panf_send.at[o, s], panf_recv.at[o, s], {"row": other})

    firsts += [pass_panels(o, 0) for o in range(1, chips)]
    for o in range(1, chips):
        cols[o - 1].wait_recv()
        share = among_cols.at[twin_share(o)]
        passed.append(send(share, share, colf_send.at[o], colf_recv.at[o], {"row": other}))
    for copy in firsts:
        copy.wait_recv()
    for copy in dealt:
        copy.wait_send()

    def halfway():
        for s in range(1, K):
            for o in range(1, chips):
                pass_panels(o, s)

    def arrived():
        late = []
        for s in range(1, K):
            for o in range(1, chips):
                part = panel_part(twin_share(o), s)
                late.append(
                    pltpu.make_async_remote_copy(
                        src_ref=part, dst_ref=part, send_sem=panf_send.at[o, s], recv_sem=panf_recv.at[o, s],
                        device_id={"row": other}, device_id_type=pl.DeviceIdType.MESH,
                    )
                )
        for copy in late + laters + passed + rows:
            copy.wait_recv()
        for group in [cols, rows, passed, firsts, laters, late] + pans + spread:
            for copy in group:
                copy.wait_send()

    run_steps(panels, shares, outs, work, total, tile, halfway, arrived)


def call(kernel, panels, covariance, data, drift, shares, scratch, **params):
    rows_here, cols_here = covariance.shape
    vmem = pl.BlockSpec(memory_space=pltpu.VMEM)
    smem = pl.BlockSpec(memory_space=pltpu.SMEM)
    return pl.pallas_call(
        kernel,
        out_shape=(
            jax.ShapeDtypeStruct((rows_here, cols_here), jnp.float32),
            jax.ShapeDtypeStruct((rows_here, K * B), jnp.float32),
            jax.ShapeDtypeStruct(data.shape, jnp.float32),
            jax.ShapeDtypeStruct(drift.shape, jnp.float32),
        ),
        in_specs=[smem] + [vmem] * (3 + len(shares)),
        out_specs=(vmem,) * 4,
        scratch_shapes=[
            pltpu.VMEM((K * B, K * B + cols_here + B + SIDES), jnp.float32),
            pltpu.VMEM((rows_here, cols_here + SIDES), jnp.float32),
            pltpu.VMEM((B, B), jnp.float32),
        ]
        + scratch,
        compiler_params=pltpu.CompilerParams(vmem_limit_bytes=56 * 1024 * 1024, **params),
        cost_estimate=pl.CostEstimate(flops=10**10, bytes_accessed=10**7, transcendentals=0),
    )(panels, covariance, data, drift, *shares)


def by_copies(layers, panels, covariance, data, drift):
    cols_here = covariance.shape[1]
    chips = SHARES // 2
    dma = pltpu.SemaphoreType.DMA
    scratch = [
        pltpu.VMEM((SHARES, K, SHARE, K * B), jnp.float32),
        pltpu.VMEM((SHARES, K, SHARE, cols_here + SIDES), jnp.float32),
        pltpu.VMEM((SHARES, K, SHARE, B), jnp.float32),
        pltpu.VMEM((SHARES, SHARE, cols_here + SIDES), jnp.float32),
    ]
    scratch += [pltpu.VMEM((2 * layers, high - low, SHARE, B), jnp.float32) for low, high in PARTS]
    scratch += [dma((SHARES,))] * 2 + [dma((layers, len(PARTS)))] * 2 + [dma((chips,))] * 4
    scratch += [dma((SHARES, len(PARTS)))] * 2 + [dma((chips, K))] * 4
    return call(
        copies_kernel, panels, covariance, data, drift, [], scratch, collective_id=0, has_side_effects=True
    )


def gather_by_sums(panels, row_tile, first_col, block):
    cols_here = block.shape[1] - SIDES
    col_tiles = cols_here // B
    mine = (panels == row_tile).astype(jnp.float32)
    rows = lax.psum((mine[:, None, None] * block[None]).reshape(K * B, -1), "row")
    parts = []
    for wanted in [panels[p] for p in range(K)] + [row_tile]:
        local = wanted - first_col
        held = (local >= 0) & (local < col_tiles)
        part = lax.dynamic_slice_in_dim(rows, jnp.clip(local, 0, col_tiles - 1) * B, B, 1)
        parts.append(jnp.where(held, part, 0.0))
    spread = lax.psum(jnp.concatenate(parts, axis=1), "col")
    return [
        part.reshape(K, SHARES, SHARE, -1).transpose(1, 0, 2, 3)
        for part in (spread[:, : K * B], rows, spread[:, K * B :])
    ]


def on_device(paired, layers, covariance, panels, observed, drift_basis):
    cols_here = covariance.shape[1]
    data = observed[None, :]
    if paired:
        complement, factor, data, drift = by_copies(layers, panels, covariance, data, drift_basis)
        return complement, factor, data[0], drift
    filler = jnp.zeros((SIDES - 1 - drift_basis.shape[0], B), jnp.float32)
    sides = jnp.concatenate([drift_basis, data, filler], axis=0)
    block = jnp.concatenate([covariance, sides.T], axis=1)
    first_col = lax.axis_index("col") * (cols_here // B)
    shares = gather_by_sums(panels, lax.axis_index("row"), first_col, block)
    complement, factor, data, drift = call(
        local_kernel, panels, covariance, data, drift_basis, shares, []
    )
    return complement, factor, data[0], drift


def solution(mesh):
    row, col = mesh.shape["row"], mesh.shape["col"]
    paired = row == SHARES and 2 * col == row
    return jax.shard_map(
        functools.partial(on_device, paired, col),
        mesh=mesh,
        in_specs=(P("row", "col"), P(), P("row"), P(None, "row")),
        out_specs=(P("row", "col"), P("row", None), P("row"), P(None, "row")),
        check_vma=False,
    )
```

time: 347 us -> 107 us (0.31); the launches traced: 343 us -> 107 us
  waiting for transfers between devices: 247 us -> 0 us
  Pallas kernels: 54.1 us -> 102 us
  other arithmetic: 17.7 us -> 0 us
  between operations: 16.7 us -> 0.65 us
    psum x2 -> x0, waiting for transfers between devices: 247 us -> none  [the longest x1 186 us: gather_panels(): spread = lax.psum(jnp.concatenate(parts, axis=1), 'col')]
    pallas_call x1, Pallas kernels: 54.1 us -> 102 us  [call(): pl.pallas_call(kernel, out_shape=(jax.ShapeDtypeStruct((rows_here, cols_h...]
    unnamed x4 -> x0, other arithmetic: 8.42 us -> none
    slice x7 -> x0, local copies, waits for them, and re-layouts: 5.97 us -> none  [the longest x2 2.78 us: on_device(): return (complement, factor, solved[0], solved[1:1 + drifts])]
    concatenate x3 -> x0, other arithmetic: 5.3 us -> none  [the longest x1 3.21 us: gather_panels(): jnp.concatenate([spread[:, :K * B], rows, spread[:, K * B:]], axis=1)]
  transfers between devices with their start and end apart: 2 -> 0, of which waited for: 2 -> 0; matrix products, arithmetic and copies ran while one was open for 0% -> 0% of each run, Pallas kernels for 0% -> 0%
where the time goes in v3:
time: 107 us
  Pallas kernels  102 us (95%)
  local copies, waits for them, and re-layouts  4.13 us (4%)
    pallas_call x1, Pallas kernels, call(): pl.pallas_call(kernel, out_shape=(jax.ShapeDtypeStruct((rows_here, cols_h...  102 us
    unnamed x10, local copies, waits for them, and re-layouts  4.13 us

profile of v3, /device:TPU:9, one launch (start us, length us, event | category | flops | bytes accessed | tf_op | source)
XLA Modules:
  0.0 107.2 jit_solution(12357146556752125660)
XLA Ops:
  0.6 102.4 %shard_map.75 = (f32[256,512]{1,0:T(8,128)}, f32[256,1024]{1,0:T(8,128)}, f32[1,256]{1,0:T(1,128)}, f32[64,256]{1,0:T(8,128)}) custom-call(s32[4]{0:T(128)} %panels.1, f32[256,512]{1,0:T(8,128)} %covariance.1, f32[1,256]{1,0:T(1,128)} %bitcast.3, f32[64,256]{1,0:T(8,128)} %drift.1), custom_call_target="tpu_custom_call" | custom-call | flops 10000000000 | bytes 10000000 | tf_op jit(solution)/shard_map/pallas_call | solution.py:318
  103.0 0.0 copy-start
  103.0 2.0 %copy.12 = f32[256,512]{1,0:T(8,128)} copy(f32[256,512]{1,0:T(8,128)} %get-tuple-element.16) | data formatting | bytes 1048576
  105.0 0.0 copy-done
  105.0 0.0 copy-start.2
  105.0 0.0 copy-start.1
  105.0 1.0 copy.13
  106.0 0.0 copy-done.2
  106.0 0.6 copy.14
  106.5 0.0 copy-done.1
  106.5 0.6 copy.15
Async XLA Ops:
  103.0 2.0 %copy-start = (f32[256,1024]{1,0:T(8,128)S(1)}, f32[256,1024]{1,0:T(8,128)}, u32[]{:S(2)}) copy-start(f32[256,1024]{1,0:T(8,128)} %get-tuple-element.17) | copy-start | bytes 3145732
  105.0 1.0 copy-start.2
  105.0 1.5 %copy-start.1 = (f32[64,256]{1,0:T(8,128)S(1)}, f32[64,256]{1,0:T(8,128)}, u32[]{:S(2)}) copy-start(f32[64,256]{1,0:T(8,128)} %get-tuple-element.19) | copy-start | bytes 196612

commit v4 on v3

--- a/solution.py
+++ b/solution.py
@@ -90,7 +90,7 @@
     return pl.ds(pl.multiple_of(index * B, B), B)
 
 
-def run_steps(panels, shares, outs, work, total, tile, halfway, arrived):
+def run_steps(panels, shares, outs, work, total, tile, halfway, arrived, rows_arrived):
     among_panels, among_cols, among_rows = shares
     complement, factor, data, drift = outs
     cols_here = complement.shape[1]
@@ -115,47 +115,81 @@
                 rows = slice(p * B + k * SHARE, p * B + (k + 1) * SHARE)
                 work[rows, p * B : K * B] = among_panels[k, p, :, p * B :]
                 work[rows, K * B : K * B + cols_here] = among_cols[k, p, :, :cols_here]
+                work[rows, tiles * B :] = among_cols[k, p, :, cols_here:]
+
+    def assemble_rows():
+        rows_arrived()
+        for p in range(K):
+            for k in range(SHARES):
+                rows = slice(p * B + k * SHARE, p * B + (k + 1) * SHARE)
                 work[rows, K * B + cols_here : tiles * B] = among_rows[k, p]
-                work[rows, tiles * B :] = among_cols[k, p, :, cols_here:]
-
-    def step(p, gone):
-        target = panels[p]
-        inverse = split(invert_factor(tile, at_first(p, halfway)))
-        at_first(p, assemble)()
-
-        def scale_tile(c, _):
-            work[tile_at(p), tile_at(c)] = product(inverse, split(work[tile_at(p), tile_at(c)]))
+
+    def gone_before(p):
+        gone = jnp.float32(0.0)
+        for s in range(K):
+            gone = jnp.where((panels[s] == row_tile) & (s < p), 1.0, gone)
+        return gone
+
+    def rows_step(p):
+        own = pl.ds((tiles - 1) * B, B)
+        here = product(split(work[tile_at(p), tile_at(p)]), split(work[tile_at(p), own]))
+        here_halves = split(here)
+
+        def update_row(q, _):
+            work[tile_at(q), own] -= product(split(work[tile_at(p), tile_at(q)].T), here_halves)
             return 0
 
-        lax.fori_loop(p + 1, tiles, scale_tile, 0)
-        side = product(inverse, split(work[tile_at(p), tail]))
-        side_halves = split(side)
-
-        def update_row(q, _):
-            turned = split(work[tile_at(p), tile_at(q)].T)
-
-            def update_tile(c, _):
-                work[tile_at(q), tile_at(c)] -= product(turned, split(work[tile_at(p), tile_at(c)]))
-                return 0
-
-            lax.fori_loop(q, tiles, update_tile, 0)
-            work[tile_at(q), tail] -= product(turned, side_halves)
-            return 0
-
         lax.fori_loop(p + 1, K, update_row, 0)
-        mine = work[tile_at(p), pl.ds((tiles - 1) * B, B)].T * (1.0 - gone)
+        mine = here.T * (1.0 - gone_before(p))
         factor[:, tile_at(p)] = mine
         turned = split(mine)
         for c in range(col_tiles):
             part = work[tile_at(p), pl.ds((K + c) * B, B)]
             total[:, c * B : (c + 1) * B] -= product(turned, split(part))
-        rest = total[:, cols_here:] - product(turned, side_halves)
-        total[:, cols_here:] = jnp.where(row_tile == target, side, rest)
+        side = work[tile_at(p), tail]
+        rest = total[:, cols_here:] - product(turned, split(side))
+        total[:, cols_here:] = jnp.where(row_tile == panels[p], side, rest)
+
+    def step(p, _):
+        exact = invert_factor(tile, at_first(p, halfway))
+        inverse = split(exact)
+        at_first(p, assemble)()
+        work[tile_at(p), tile_at(p)] = exact
+
+        def scale_tile(c, _):
+            work[tile_at(p), tile_at(c)] = product(inverse, split(work[tile_at(p), tile_at(c)]))
+            return 0
+
+        lax.fori_loop(p + 1, tiles - 1, scale_tile, 0)
+        side = product(inverse, split(work[tile_at(p), tail]))
+        side_halves = split(side)
+        work[tile_at(p), tail] = side
+
+        def update_row(q, _):
+            turned = split(work[tile_at(p), tile_at(q)].T)
+
+            def update_tile(c, _):
+                work[tile_at(q), tile_at(c)] -= product(turned, split(work[tile_at(p), tile_at(c)]))
+                return 0
+
+            lax.fori_loop(q, tiles - 1, update_tile, 0)
+            work[tile_at(q), tail] -= product(turned, side_halves)
+            return 0
+
+        lax.fori_loop(p + 1, K, update_row, 0)
+
+        def lagging():
+            pl.when(p == 1)(assemble_rows)
+            rows_step(p - 1)
+
+        pl.when(p > 0)(lagging)
         following = jnp.minimum(p + 1, K - 1)
         tile[...] = work[tile_at(following), tile_at(following)]
-        return jnp.where(row_tile == target, 1.0, gone)
-
-    gone = lax.fori_loop(0, K, step, jnp.float32(0.0))
+        return 0
+
+    lax.fori_loop(0, K, step, 0)
+    rows_step(K - 1)
+    gone = gone_before(K)
     for c in range(col_tiles):
         keep = 1.0 - gone
         for p in range(K):
@@ -176,7 +210,7 @@
 def local_kernel(panels, covariance, data, drift, *refs):
     shares, outs, (work, total, tile) = refs[:3], refs[3:7], refs[7:]
     stack_block(covariance, data, drift, total)
-    run_steps(panels, shares, outs, work, total, tile, lambda: None, lambda: None)
+    run_steps(panels, shares, outs, work, total, tile, *[lambda: None] * 3)
 
 
 def copies_kernel(panels, covariance, data, drift, *refs):
@@ -302,13 +336,19 @@
                         device_id={"row": other}, device_id_type=pl.DeviceIdType.MESH,
                     )
                 )
-        for copy in late + laters + passed + rows:
+        for copy in late + laters + passed:
             copy.wait_recv()
-        for group in [cols, rows, passed, firsts, laters, late] + pans + spread:
+        for group in [cols, passed, firsts, laters, late] + pans + spread:
             for copy in group:
                 copy.wait_send()
 
-    run_steps(panels, shares, outs, work, total, tile, halfway, arrived)
+    def rows_arrived():
+        for copy in rows:
+            copy.wait_recv()
+        for copy in rows:
+            copy.wait_send()
+
+    run_steps(panels, shares, outs, work, total, tile, halfway, arrived, rows_arrived)
 
 
 def call(kernel, panels, covariance, data, drift, shares, scratch, **params):

time: 107 us -> 101 us (0.944); the launches traced: 107 us -> 99.8 us
  Pallas kernels: 102 us -> 95 us
    pallas_call x1, Pallas kernels: 102 us -> 95 us  [call(): pl.pallas_call(kernel, out_shape=(jax.ShapeDtypeStruct((rows_here, cols_h...]
where the time goes in v4:
time: 101 us; the launch traced here: 99.8 us
  Pallas kernels  95 us (94%)
  local copies, waits for them, and re-layouts  4.13 us (4%)
    pallas_call x1, Pallas kernels, call(): pl.pallas_call(kernel, out_shape=(jax.ShapeDtypeStruct((rows_here, cols_h...  95 us
    unnamed x10, local copies, waits for them, and re-layouts  4.13 us

profile of v4, /device:TPU:9, one launch (start us, length us, event | category | flops | bytes accessed | tf_op | source)
XLA Modules:
  0.0 99.8 jit_solution(8535446421066596794)
XLA Ops:
  0.6 95.0 %shard_map.75 = (f32[256,512]{1,0:T(8,128)}, f32[256,1024]{1,0:T(8,128)}, f32[1,256]{1,0:T(1,128)}, f32[64,256]{1,0:T(8,128)}) custom-call(s32[4]{0:T(128)} %panels.1, f32[256,512]{1,0:T(8,128)} %covariance.1, f32[1,256]{1,0:T(1,128)} %bitcast.3, f32[64,256]{1,0:T(8,128)} %drift.1), custom_call_target="tpu_custom_call" | custom-call | flops 10000000000 | bytes 10000000 | tf_op jit(solution)/shard_map/pallas_call | solution.py:358
  95.7 0.0 copy-start
  95.7 2.0 %copy.12 = f32[256,512]{1,0:T(8,128)} copy(f32[256,512]{1,0:T(8,128)} %get-tuple-element.16) | data formatting | bytes 1048576
  97.6 0.0 copy-done
  97.6 0.0 copy-start.2
  97.6 0.0 copy-start.1
  97.6 1.0 copy.13
  98.6 0.0 copy-done.2
  98.6 0.6 copy.14
  99.2 0.0 copy-done.1
  99.2 0.6 copy.15
Async XLA Ops:
  95.7 2.0 %copy-start = (f32[256,1024]{1,0:T(8,128)S(1)}, f32[256,1024]{1,0:T(8,128)}, u32[]{:S(2)}) copy-start(f32[256,1024]{1,0:T(8,128)} %get-tuple-element.17) | copy-start | bytes 3145732
  97.6 1.0 copy-start.2
  97.6 1.5 %copy-start.1 = (f32[64,256]{1,0:T(8,128)S(1)}, f32[64,256]{1,0:T(8,128)}, u32[]{:S(2)}) copy-start(f32[64,256]{1,0:T(8,128)} %get-tuple-element.19) | copy-start | bytes 196612
